TPU v7x, 128 devices: a whole 4x4x4 slice. The times are simulated.
128 devices in a mesh: gx: 4 (over y_lo, core), gy: 4 (over z), gz: 8 (over x, y_hi).
Axes of the slice: x: 4, y: 4 (y_hi: 2, y_lo: 2; y = y_hi * 2 + y_lo), z: 4, core: 2. Of those that a mesh axis runs over, the one named last changes fastest.
Arguments:
- wave_bands: bfloat16 [96, 96, 256, 256], P('gx', 'gy', 'gz'), may hold values from -6 to 6
- potential: float32 [32, 32, 128], P('gx', 'gy', 'gz'), may hold values from -1 to 1
- occupation: float32 [4, 4, 8, 256], P('gx', 'gy', 'gz'), may hold values from 0.001 to 0.008
- support: float32 [96, 96, 256], P('gx', 'gy', 'gz'), may hold values from 0.25 to 1
- z_cuts: int32 [9], replicated, may hold values from 0 to 128, as said below
- atom_state: float32 [4, 16384], P(None, ('gx', 'gy', 'gz')), may hold values from -6 to 6
- atom_cell: int32 [16384], P(('gx', 'gy', 'gz')), may hold values from 0 to 127, as said below
Outputs:
- density: float32 [32, 32, 128], P('gx', 'gy', 'gz')
- new_bands: bfloat16 [96, 96, 320, 256], P('gx', 'gy', 'gz')
- new_atoms: float32 [4, 32768], P(None, ('gx', 'gy', 'gz'))
- new_cells: int32 [32768], P(('gx', 'gy', 'gz'))
Inputs may be any that keep to these rules, and one draw needn't show every extreme that they name: `z_cuts`: entry k is k * 16 plus an offset from 0 to 8; the first and the last offsets are 0; where there are two or more interior cuts, some offset is exactly 8. `atom_cell`: the atoms of a domain with z index c lie in cells c * 16 to c * 16 + 15.
All inputs are finite; a program needn't handle non-finite values.
Results may differ from a plain program's by a relative error of at most 0.012.
Values may be sent and summed in bfloat16 or wider, within the bound.
No kernel may reach another device: no remote copies, remote signals or barrier semaphores. Data moves between devices by JAX's collectives and lax.ppermute only.
A program may use at most 192 MiB of HBM per device.

v0:
```python
import jax
import jax.numpy as jnp
from jax import lax
from jax.sharding import PartitionSpec as P

B = 8
SWEEPS = 2
COMP = 4
CZ = 16
DRIFT = 8
DZCAP = 40
ACAP = 256


step_size = 0.08


def padded_2(shard, sides, width):
    for axis, dim in sides:
        size, length = (lax.axis_size(axis), shard.shape[dim])
        up = [(i, (i + 1) % size) for i in range(size)]
        down = [(j, i) for i, j in up]
        last = lax.slice_in_dim(shard, length - width, length, axis=dim)
        leading = lax.slice_in_dim(shard, 0, width, axis=dim)
        before = lax.ppermute(last, axis, up)
        after = lax.ppermute(leading, axis, down)
        shard = jnp.concatenate([before, shard, after], axis=dim)
    return shard


def from_behind(shard, axis, by):
    size = lax.axis_size(axis)
    pairs = [(i, i + by) for i in range(size) if 0 <= i + by < size]
    return lax.ppermute(shard, axis, pairs)


def kinetic(values):
    padded = jnp.pad(values, ((2, 2), (2, 2), (2, 2), (0, 0)))
    centre = padded[2:-2, 2:-2, 2:-2]
    far_sum = (
        padded[4:, 2:-2, 2:-2]
        + padded[:-4, 2:-2, 2:-2]
        + padded[2:-2, 4:, 2:-2]
        + padded[2:-2, :-4, 2:-2]
        + padded[2:-2, 2:-2, 4:]
        + padded[2:-2, 2:-2, :-4]
    )
    near_sum = (
        padded[3:-1, 2:-2, 2:-2]
        + padded[1:-3, 2:-2, 2:-2]
        + padded[2:-2, 3:-1, 2:-2]
        + padded[2:-2, 1:-3, 2:-2]
        + padded[2:-2, 2:-2, 3:-1]
        + padded[2:-2, 2:-2, 1:-3]
    )
    laplace = (16.0 * near_sum - far_sum - 90.0 * centre) / 12.0
    return -0.5 * laplace


def relax_sweep(wave_set, local_potential):
    values = wave_set.astype(jnp.float32)
    update = kinetic(values) + local_potential[:, :, :, None] * values
    return (values - step_size * update).astype(jnp.bfloat16)


def fold_axis(extended, axis_dim):
    inner_size = extended.shape[axis_dim] - 4 * B
    inside = lax.slice_in_dim(extended, 2 * B, 2 * B + inner_size, axis=axis_dim)
    below_rim = lax.slice_in_dim(extended, 0, B, axis=axis_dim)
    above_rim = lax.slice_in_dim(extended, inner_size + 3 * B, inner_size + 4 * B, axis=axis_dim)
    below_pad = [(0, 0), (0, 0), (0, 0)]
    above_pad = [(0, 0), (0, 0), (0, 0)]
    below_pad[axis_dim] = (0, inner_size - B)
    above_pad[axis_dim] = (inner_size - B, 0)
    return inside + jnp.pad(below_rim, below_pad) + jnp.pad(above_rim, above_pad)


def slot_table(slots, count):
    return slots[:, None] == jnp.arange(count, dtype=jnp.int32)[None, :]


def place_rows(state_rows, table):
    return jnp.dot(
        state_rows,
        table.astype(jnp.float32),
        precision=lax.Precision.HIGHEST,
        preferred_element_type=jnp.float32,
    )


def place_cells(cells, table):
    return jnp.sum(jnp.where(table, (cells + 1)[:, None], 0), axis=0)


def local(wave_bands, potential, occupation, support, z_cuts, atom_state, atom_cell):
    band_count = wave_bands.shape[3]
    atom_slots = atom_cell.shape[0]
    slab_index = lax.axis_index("gz")
    local_potential = padded_2(potential, (("gx", 0), ("gy", 1), ("gz", 2)), B)
    wave_set = wave_bands
    for sweep_index in range(SWEEPS):
        wave_set = relax_sweep(wave_set, local_potential)
    upper_rows = lax.slice_in_dim(wave_set, 2 * B, 2 * B + DRIFT, axis=2)
    next_rows = from_behind(upper_rows, "gz", -1)
    band_weights = occupation.reshape(band_count)
    values = wave_set.astype(jnp.float32)
    domain_density = support * jnp.sum(values * values * band_weights, axis=-1)
    extended = padded_2(
        domain_density.astype(jnp.bfloat16), (("gx", 0), ("gy", 1), ("gz", 2)), B
    ).astype(domain_density.dtype)
    density = fold_axis(fold_axis(fold_axis(extended, 0), 1), 2)
    padding = jnp.zeros((wave_set.shape[0], wave_set.shape[1], DRIFT, band_count), jnp.bfloat16)
    joined = jnp.concatenate([wave_set, next_rows, padding], axis=2)
    start_row = z_cuts[slab_index] - slab_index * CZ
    window = lax.dynamic_slice_in_dim(joined, start_row, DZCAP, axis=2)
    extent = z_cuts[slab_index + 1] - z_cuts[slab_index] + 2 * B
    keep_rows = jnp.arange(DZCAP, dtype=jnp.int32) < extent
    new_bands = jnp.where(keep_rows[None, None, :, None], window, jnp.zeros((), jnp.bfloat16))
    staying = atom_cell >= z_cuts[slab_index]
    leaving = jnp.logical_not(staying)
    leave_slot = jnp.where(leaving, jnp.cumsum(leaving.astype(jnp.int32)) - 1, atom_slots)
    leave_table = slot_table(leave_slot, atom_slots)
    with_cells = jnp.concatenate([atom_state, (atom_cell + 1).astype(jnp.float32)[None, :]], axis=0)
    packed = place_rows(with_cells, leave_table)
    arrivals = from_behind(packed, "gz", -1)
    arrival_cells = arrivals[COMP].astype(jnp.int32) - 1
    arriving = arrival_cells >= 0
    stay_slot = jnp.where(staying, jnp.cumsum(staying.astype(jnp.int32)) - 1, ACAP)
    stay_total = jnp.sum(staying.astype(jnp.int32))
    arrive_slot = jnp.where(arriving, stay_total + jnp.cumsum(arriving.astype(jnp.int32)) - 1, ACAP)
    stay_table = slot_table(stay_slot, ACAP)
    arrive_table = slot_table(arrive_slot, ACAP)
    new_atoms = place_rows(atom_state, stay_table) + place_rows(arrivals[:COMP], arrive_table)
    new_cells = place_cells(atom_cell, stay_table) + place_cells(arrival_cells, arrive_table) - 1
    return (density, new_bands, new_atoms, new_cells)


def solution(mesh):
    in_specs = (
        P("gx", "gy", "gz", None),
        P("gx", "gy", "gz"),
        P("gx", "gy", "gz", None),
        P("gx", "gy", "gz"),
        P(),
        P(None, ("gx", "gy", "gz")),
        P(("gx", "gy", "gz")),
    )
    out_specs = (
        P("gx", "gy", "gz"),
        P("gx", "gy", "gz", None),
        P(None, ("gx", "gy", "gz")),
        P(("gx", "gy", "gz")),
    )
    return jax.shard_map(local, mesh=mesh, in_specs=in_specs, out_specs=out_specs, check_vma=False)
```

profile of v0, /device:TPU:22, one launch (start us, length us, event | category | flops | bytes accessed | tf_op | source)
XLA Modules:
  0.0 358.8 jit_solution(8038601748807856132)
XLA Ops:
  0.6 0.0 copy-start.1
  0.6 0.1 collective-permute-start
  0.7 1.7 collective-permute-start.1
  2.5 1.3 fusion.57
  3.8 1.9 broadcast_add_fusion
  5.7 0.1 copy.18
  5.8 0.2 reduce-window.27
  6.0 0.1 copy.17
  6.1 0.2 reduce-window.26
  6.3 0.1 add_reduce_fusion.1
  6.4 0.9 fusion.42
  7.3 2.3 collective-permute-start.13
  11.5 0.9 convolution_bitcast_fusion
  12.4 0.1 select_reduce_fusion.1
  12.5 0.1 pad_dynamic-slice_fusion.2
  12.6 12.7 %convert_element_type.72 = f32[24,24,32,256]{3,2,1,0:T(8,128)} convert(bf16[24,24,32,256]{3,2,1,0:T(8,128)(2,1)} %param.7) | non-fusion elementwise | flops 4718592 | bytes 28311552 | tf_op jit(solution)/shard_map/convert_element_type | solution.py:61
  25.3 0.0 collective-permute-done.13
  25.3 0.1 copy.19
  25.4 0.2 reduce-window.28
  25.6 0.0 collective-permute-done
  25.6 0.0 copy-done.1
  25.6 0.0 collective-permute-done.1
  25.7 4.1 %collective-permute-start.3 = (f32[24,8,16]{2,1,0:T(8,128)S(1)}, f32[24,8,16]{2,1,0:T(8,128)S(1)}, u32[]{:S(2)}, u32[]{:S(2)}) collective-permute-start(f32[24,8,16]{2,1,0:T(8,128)S(1)} %constant_dynamic-update-slice_fusion), channel_id=1, source_target_pairs={{8,0},{16,8},{24,16},{0,24},{9,1},{17,9},{25,17},{1,25},{10,2},{18... | collective-permute-start | bytes 36872 | tf_op jit(solution)/shard_map/ppermute | solution.py:26
  29.8 0.0 collective-permute-start.2
  29.8 0.7 add_reduce_fusion
  30.5 1.5 collective-permute-done.3
  32.0 3.6 %collective-permute-done.2 = f32[24,8,16]{2,1,0:T(8,128)S(1)} collective-permute-done((f32[24,8,16]{2,1,0:T(8,128)S(1)}, f32[24,8,16]{2,1,0:T(8,128)S(1)}, u32[]{:S(2)}, u32[]{:S(2)}) %collective-permute-start.2) | collective-permute-done | bytes 12320 | tf_op jit(solution)/shard_map/ppermute | solution.py:25
  35.6 0.1 fusion.55
  35.8 3.5 collective-permute-start.5
  39.3 2.2 collective-permute-start.4
  41.5 8.5 %collective-permute-done.5 = f32[24,24,8]{2,1,0:T(8,128)S(1)} collective-permute-done((f32[24,24,8]{2,1,0:T(8,128)S(1)}, f32[24,24,8]{2,1,0:T(8,128)S(1)}, u32[]{:S(2)}, u32[]{:S(2)}) %collective-permute-start.5) | collective-permute-done | bytes 18464 | tf_op jit(solution)/shard_map/ppermute | solution.py:26
  50.0 2.9 collective-permute-done.4
  52.9 0.2 pad_maximum_fusion.2
  53.1 0.0 copy-start.2
  53.2 100.6 %fusion.39 = f32[24,24,32,256]{3,2,1,0:T(8,128)} fusion(f32[24,24,32,256]{3,2,1,0:T(8,128)} %convert_element_type.72, f32[24,24,32]{2,1,0:T(8,128)S(1)} %pad_maximum_fusion.2), kind=kLoop, calls=%fused_computation.66 | loop fusion | flops 99090432 | bytes 37822464 | tf_op jit(solution)/shard_map/convert_element_type | solution.py:61
  153.8 0.0 copy-done.2
  153.8 0.0 copy-start.3
  153.8 106.9 %multiply_reduce_fusion = (f32[24,24,32]{2,1,0:T(8,128)S(1)}, bf16[24,24,32,256]{3,2,1,0:T(8,128)(2,1)}) fusion(f32[256]{0:T(256)S(1)} %bitcast.18, f32[24,24,32,256]{3,2,1,0:T(8,128)} %fusion.39, f32[24,24,32]{2,1,0:T(8,128)S(1)} %pad_maximum_fusion.2), kind=kLoop, calls=%fused_computation.58 | loop fusion | flops 113227776 | bytes 28460032 | tf_op jit(solution)/shard_map/reduce_sum | solution.py:107
  260.7 1.8 slice.194
  262.5 3.1 collective-permute-start.12
  265.6 0.8 convolution_add_fusion
  266.4 0.0 copy-done
  266.5 0.3 collective-permute-start.7
  266.8 0.5 collective-permute-start.6
  267.3 48.6 %collective-permute-done.7 = bf16[8,24,32]{2,1,0:T(8,128)(2,1)S(1)} collective-permute-done((bf16[8,24,32]{2,1,0:T(8,128)(2,1)S(1)}, bf16[8,24,32]{2,1,0:T(8,128)(2,1)S(1)}, u32[]{:S(2)}, u32[]{:S(2)}) %collective-permute-start.7) | collective-permute-done | bytes 12320 | tf_op jit(solution)/shard_map/ppermute | solution.py:26
  315.9 0.0 collective-permute-done.6
  315.9 0.4 collective-permute-start.9
  316.3 1.7 collective-permute-start.8
  318.0 0.1 select_reduce_fusion
  318.1 2.9 collective-permute-done.9
  321.0 1.4 collective-permute-done.8
  322.4 0.1 pad_maximum_fusion
  322.5 0.2 fusion.54
  322.7 0.1 collective-permute-start.11
  322.8 5.6 %collective-permute-start.10 = (bf16[40,40,8]{2,1,0:T(8,128)(2,1)S(1)}, bf16[40,40,8]{2,1,0:T(8,128)(2,1)S(1)}, u32[]{:S(2)}, u32[]{:S(2)}) collective-permute-start(bf16[40,40,8]{2,1,0:T(8,128)(2,1)S(1)} %get-tuple-element.8), channel_id=1, source_target_pairs={{0,1},{1,2},{2,3},{3,4},{4,5},{5,6},{6,7},{7,0},{8,9},{9,10},{10,1... | collective-permute-start | bytes 76808 | tf_op jit(solution)/shard_map/ppermute | solution.py:25
  328.4 0.6 add_add_fusion
  329.0 11.5 %collective-permute-done.11 = bf16[40,40,8]{2,1,0:T(8,128)(2,1)S(1)} collective-permute-done((bf16[40,40,8]{2,1,0:T(8,128)(2,1)S(1)}, bf16[40,40,8]{2,1,0:T(8,128)(2,1)S(1)}, u32[]{:S(2)}, u32[]{:S(2)}) %collective-permute-start.11) | collective-permute-done | bytes 25632 | tf_op jit(solution)/shard_map/ppermute | solution.py:26
  340.5 4.0 %collective-permute-done.10 = bf16[40,40,8]{2,1,0:T(8,128)(2,1)S(1)} collective-permute-done((bf16[40,40,8]{2,1,0:T(8,128)(2,1)S(1)}, bf16[40,40,8]{2,1,0:T(8,128)(2,1)S(1)}, u32[]{:S(2)}, u32[]{:S(2)}) %collective-permute-start.10) | collective-permute-done | bytes 25632 | tf_op jit(solution)/shard_map/ppermute | solution.py:25
  344.5 0.4 maximum_convert_fusion
  344.9 0.1 slice.193
  345.0 0.0 copy-done.3
  345.0 0.7 fusion.44
  345.7 0.0 collective-permute-done.12
  345.7 13.1 %fusion.38 = bf16[24,24,40,256]{3,2,1,0:T(8,128)(2,1)} fusion(s32[]{:T(128)S(6)} %select_n.38, bf16[24,24,32,256]{3,2,1,0:T(8,128)(2,1)} %get-tuple-element.7, bf16[24,24,8,256]{3,2,1,0:T(8,128)(2,1)S(1)} %collective-permute-done.12, pred[40]{0:T(512)(128)(4,1)S(1)} %iota_compare_fusion.6, bf16[40]{0:T(256)(128)(2,1)S(1)} %pad_dynamic-slice_fusion.2), kind=kLoop, calls=%fused_computation.65 | loop fusion | flops 41287680 | bytes 23593084 | tf_op jit(solution)/shard_map/jit(_where)/select_n | solution.py:118
  (17 shorter events, 0.2 us)
Async XLA Ops:
  0.6 25.0 %copy-start.1 = (f32[8,8,16]{2,1,0:T(8,128)S(1)}, f32[8,8,16]{2,1,0:T(8,128)}, u32[]{:S(2)}) copy-start(f32[8,8,16]{2,1,0:T(8,128)} %param.8) | copy-start | bytes 12292
  0.6 25.0 %collective-permute-start = (f32[8,8,16]{2,1,0:T(8,128)}, f32[8,8,16]{2,1,0:T(8,128)S(1)}, u32[]{:S(2)}, u32[]{:S(2)}) collective-permute-start(f32[8,8,16]{2,1,0:T(8,128)} %param.8), channel_id=1, source_target_pairs={{0,32},{32,64},{64,96},{96,0},{1,33},{33,65},{65,97},{97,1},{2,34}... | collective-permute-start | bytes 12296 | tf_op jit(solution)/shard_map/ppermute | solution.py:25
  0.7 24.9 %collective-permute-start.1 = (f32[8,8,16]{2,1,0:T(8,128)}, f32[8,8,16]{2,1,0:T(8,128)S(1)}, u32[]{:S(2)}, u32[]{:S(2)}) collective-permute-start(f32[8,8,16]{2,1,0:T(8,128)} %param.8), channel_id=1, source_target_pairs={{32,0},{64,32},{96,64},{0,96},{33,1},{65,33},{97,65},{1,97},{34,2}... | collective-permute-start | bytes 12296 | tf_op jit(solution)/shard_map/ppermute | solution.py:26
  7.3 18.0 %collective-permute-start.13 = (f32[5,128]{1,0:T(8,128)S(1)}, f32[5,128]{1,0:T(8,128)S(1)}, u32[]{:S(2)}, u32[]{:S(2)}) collective-permute-start(f32[5,128]{1,0:T(8,128)S(1)} %fusion.42), channel_id=1, source_target_pairs={{1,0},{2,1},{3,2},{4,3},{5,4},{6,5},{7,6},{9,8},{10,9},{11,10},{12... | collective-permute-start | bytes 7688 | tf_op jit(solution)/shard_map/ppermute | solution.py:34
  25.7 6.3 %collective-permute-start.3 = (f32[24,8,16]{2,1,0:T(8,128)S(1)}, f32[24,8,16]{2,1,0:T(8,128)S(1)}, u32[]{:S(2)}, u32[]{:S(2)}) collective-permute-start(f32[24,8,16]{2,1,0:T(8,128)S(1)} %constant_dynamic-update-slice_fusion), channel_id=1, source_target_pairs={{8,0},{16,8},{24,16},{0,24},{9,1},{17,9},{25,17},{1,25},{10,2},{18... | collective-permute-start | bytes 36872 | tf_op jit(solution)/shard_map/ppermute | solution.py:26
  29.8 5.8 %collective-permute-start.2 = (f32[24,8,16]{2,1,0:T(8,128)S(1)}, f32[24,8,16]{2,1,0:T(8,128)S(1)}, u32[]{:S(2)}, u32[]{:S(2)}) collective-permute-start(f32[24,8,16]{2,1,0:T(8,128)S(1)} %constant_dynamic-update-slice_fusion), channel_id=1, source_target_pairs={{0,8},{8,16},{16,24},{24,0},{1,9},{9,17},{17,25},{25,1},{2,10},{10... | collective-permute-start | bytes 36872 | tf_op jit(solution)/shard_map/ppermute | solution.py:25
  35.8 14.2 %collective-permute-start.5 = (f32[24,24,8]{2,1,0:T(8,128)S(1)}, f32[24,24,8]{2,1,0:T(8,128)S(1)}, u32[]{:S(2)}, u32[]{:S(2)}) collective-permute-start(f32[24,24,8]{2,1,0:T(8,128)S(1)} %get-tuple-element.11), channel_id=1, source_target_pairs={{1,0},{2,1},{3,2},{4,3},{5,4},{6,5},{7,6},{0,7},{9,8},{10,9},{11,1... | collective-permute-start | bytes 55304 | tf_op jit(solution)/shard_map/ppermute | solution.py:26
  39.3 13.6 %collective-permute-start.4 = (f32[24,24,8]{2,1,0:T(8,128)S(1)}, f32[24,24,8]{2,1,0:T(8,128)S(1)}, u32[]{:S(2)}, u32[]{:S(2)}) collective-permute-start(f32[24,24,8]{2,1,0:T(8,128)S(1)} %get-tuple-element.10), channel_id=1, source_target_pairs={{0,1},{1,2},{2,3},{3,4},{4,5},{5,6},{6,7},{7,0},{8,9},{9,10},{10,1... | collective-permute-start | bytes 55304 | tf_op jit(solution)/shard_map/ppermute | solution.py:25
  53.1 100.6 %copy-start.2 = (f32[1,1,1,256]{3,2,1,0:T(1,128)S(1)}, f32[1,1,1,256]{3,2,1,0:T(1,128)}, u32[]{:S(2)}) copy-start(f32[1,1,1,256]{3,2,1,0:T(1,128)} %param.9) | copy-start | bytes 3076
  153.8 112.7 %copy-start = (f32[24,24,32]{2,1,0:T(8,128)S(1)}, f32[24,24,32]{2,1,0:T(8,128)}, u32[]{:S(2)}) copy-start(f32[24,24,32]{2,1,0:T(8,128)} %param.10) | copy-start | bytes 221188
  153.8 191.2 %copy-start.3 = (pred[16]{0:T(512)(128)(4,1)S(1)}, pred[16]{0:T(512)(128)(4,1)}, u32[]{:S(2)}) copy-start(pred[16]{0:T(512)(128)(4,1)} %constant.44.clone.1) | copy-start | bytes 52
  262.5 83.2 %collective-permute-start.12 = (bf16[24,24,8,256]{3,2,1,0:T(8,128)(2,1)S(1)}, bf16[24,24,8,256]{3,2,1,0:T(8,128)(2,1)S(1)}, u32[]{:S(2)}, u32[]{:S(2)}) collective-permute-start(bf16[24,24,8,256]{3,2,1,0:T(8,128)(2,1)S(1)} %slice.194), channel_id=1, source_target_pairs={{1,0},{2,1},{3,2},{4,3},{5,4},{6,5},{7,6},{9,8},{10,9},{11,10},{12... | collective-permute-start | bytes 7077896 | tf_op jit(solution)/shard_map/ppermute | solution.py:34
  266.5 49.4 %collective-permute-start.7 = (bf16[8,24,32]{2,1,0:T(8,128)(2,1)S(1)}, bf16[8,24,32]{2,1,0:T(8,128)(2,1)S(1)}, u32[]{:S(2)}, u32[]{:S(2)}) collective-permute-start(bf16[8,24,32]{2,1,0:T(8,128)(2,1)S(1)} %get-tuple-element.15), channel_id=1, source_target_pairs={{32,0},{64,32},{96,64},{0,96},{33,1},{65,33},{97,65},{1,97},{34,2}... | collective-permute-start | bytes 36872 | tf_op jit(solution)/shard_map/ppermute | solution.py:26
  266.8 49.1 %collective-permute-start.6 = (bf16[8,24,32]{2,1,0:T(8,128)(2,1)S(1)}, bf16[8,24,32]{2,1,0:T(8,128)(2,1)S(1)}, u32[]{:S(2)}, u32[]{:S(2)}) collective-permute-start(bf16[8,24,32]{2,1,0:T(8,128)(2,1)S(1)} %get-tuple-element.14), channel_id=1, source_target_pairs={{0,32},{32,64},{64,96},{96,0},{1,33},{33,65},{65,97},{97,1},{2,34}... | collective-permute-start | bytes 36872 | tf_op jit(solution)/shard_map/ppermute | solution.py:25
  315.9 5.1 %collective-permute-start.9 = (bf16[40,8,32]{2,1,0:T(8,128)(2,1)S(1)}, bf16[40,8,32]{2,1,0:T(8,128)(2,1)S(1)}, u32[]{:S(2)}, u32[]{:S(2)}) collective-permute-start(bf16[40,8,32]{2,1,0:T(8,128)(2,1)S(1)} %get-tuple-element.13), channel_id=1, source_target_pairs={{8,0},{16,8},{24,16},{0,24},{9,1},{17,9},{25,17},{1,25},{10,2},{18... | collective-permute-start | bytes 61448 | tf_op jit(solution)/shard_map/ppermute | solution.py:26
  316.3 6.2 %collective-permute-start.8 = (bf16[40,8,32]{2,1,0:T(8,128)(2,1)S(1)}, bf16[40,8,32]{2,1,0:T(8,128)(2,1)S(1)}, u32[]{:S(2)}, u32[]{:S(2)}) collective-permute-start(bf16[40,8,32]{2,1,0:T(8,128)(2,1)S(1)} %get-tuple-element.12), channel_id=1, source_target_pairs={{0,8},{8,16},{16,24},{24,0},{1,9},{9,17},{17,25},{25,1},{2,10},{10... | collective-permute-start | bytes 61448 | tf_op jit(solution)/shard_map/ppermute | solution.py:25
  322.7 17.8 %collective-permute-start.11 = (bf16[40,40,8]{2,1,0:T(8,128)(2,1)S(1)}, bf16[40,40,8]{2,1,0:T(8,128)(2,1)S(1)}, u32[]{:S(2)}, u32[]{:S(2)}) collective-permute-start(bf16[40,40,8]{2,1,0:T(8,128)(2,1)S(1)} %get-tuple-element.9), channel_id=1, source_target_pairs={{1,0},{2,1},{3,2},{4,3},{5,4},{6,5},{7,6},{0,7},{9,8},{10,9},{11,1... | collective-permute-start | bytes 76808 | tf_op jit(solution)/shard_map/ppermute | solution.py:26
  322.8 21.7 %collective-permute-start.10 = (bf16[40,40,8]{2,1,0:T(8,128)(2,1)S(1)}, bf16[40,40,8]{2,1,0:T(8,128)(2,1)S(1)}, u32[]{:S(2)}, u32[]{:S(2)}) collective-permute-start(bf16[40,40,8]{2,1,0:T(8,128)(2,1)S(1)} %get-tuple-element.8), channel_id=1, source_target_pairs={{0,1},{1,2},{2,3},{3,4},{4,5},{5,6},{6,7},{7,0},{8,9},{9,10},{10,1... | collective-permute-start | bytes 76808 | tf_op jit(solution)/shard_map/ppermute | solution.py:25
where the time goes:
time: 361 us; the launch traced here: 359 us
  other arithmetic  239 us (66%)
  waiting for transfers between devices  85 us (24%)
  starting transfers between devices  25.6 us (7%)
  local copies, waits for them, and re-layouts  4.01 us (1%)
    convert_element_type x2, other arithmetic, relax_sweep(): values = wave_set.astype(jnp.float32)  113 us
    reduce_sum x1, other arithmetic, local(): domain_density = support * jnp.sum(values * values * band_weights, axis=-1)  107 us
    ppermute x6, waiting for transfers between devices, padded_2(): after = lax.ppermute(leading, axis, down)  73 us
    select_n x1, other arithmetic, local(): jnp.where(keep_rows[None, None, :, None], window, jnp.zeros((), jnp.bfloa...  13.1 us
    ppermute x6, waiting for transfers between devices, padded_2(): before = lax.ppermute(last, axis, up)  12 us
    ppermute x6, starting transfers between devices, padded_2(): before = lax.ppermute(last, axis, up)  10.1 us
    ppermute x6, starting transfers between devices, padded_2(): after = lax.ppermute(leading, axis, down)  10.1 us
  transfers between devices with their start and end apart: 14, of which 9 were waited for; matrix products, arithmetic and copies ran while one was open for 6% of the time, Pallas kernels for 0%

commit v1 on v0

v1 whole, which is shorter than its diff:
```python
import functools
import numpy as np
import jax
import jax.numpy as jnp
from jax import lax
from jax.experimental import pallas as pl
from jax.experimental.pallas import tpu as pltpu
from jax.sharding import PartitionSpec as P
import ml_dtypes

B = 8
COMP = 4
CX = 8
CZ = 16
DX = 24
DZ = 32
DRIFT = 8
DZCAP = 40
ACAP = 256
NB = 256
N_GX = 4
N_GY = 4
N_GZ = 8
YB = 8
YR = 6
ROWS = YB * DZ
PLANE = DX * DZ
RING = 8
VMEM_BYTES = 48 * 1024 * 1024

CENTRE = 210.0 / 16.0
FAR = 1.0 / 16.0
POT = -24.0 / 16.0
SCALE = 16.0 / 300.0

CHUNKS = (((0, 4),), ((4, 8), (8, 12)), ((12, 16), (16, 20), (20, 24)))


def stencil_matrix():
    out = np.zeros((YB + 4, DZ, YB, DZ), np.float32)
    for y in range(YB + 4):
        for k in range(YB):
            gap = abs(y - 2 - k)
            for z in range(DZ):
                if gap == 0:
                    out[y, z, k, z] = CENTRE
                    for step, value in ((1, 1.0), (2, -FAR)):
                        for side in (z - step, z + step):
                            if 0 <= side < DZ:
                                out[y, z, k, side] = value
                elif gap == 1:
                    out[y, z, k, z] = 1.0
                elif gap == 2:
                    out[y, z, k, z] = -FAR
    return out.reshape((YB + 4) * DZ, ROWS).astype(ml_dtypes.bfloat16)


def sweep_pieces(ring, matrix_ref, x):
    here = ring[x & 7]
    cells = jnp.concatenate([here[ROWS * block : ROWS * block + ROWS] for block in range(3)], axis=1)
    product = jnp.dot(matrix_ref[...], cells, preferred_element_type=jnp.float32)

    def part(block, row):
        return product[row : row + 64, NB * block : NB * block + NB]

    for piece in range(12):
        block, inner = divmod(piece, 4)
        total = part(block, 64 + 64 * inner)
        if inner == 3 and block < 2:
            total = total + part(block + 1, 0)
        if inner == 0 and block > 0:
            total = total + part(block - 1, 320)
        rows = slice(64 * piece, 64 * piece + 64)
        near = ring[(x - 1) & 7, rows] + ring[(x + 1) & 7, rows]
        far = ring[(x - 2) & 7, rows] + ring[(x + 2) & 7, rows]
        yield piece, rows, total, near - far * jnp.bfloat16(FAR)


def clear_outside(ring, first, plane):
    if first == 0:

        @pl.when(pl.program_id(0) == 0)
        def _():
            ring[RING - 2] = jnp.zeros_like(ring[0])
            ring[RING - 1] = jnp.zeros_like(ring[0])

    @pl.when(plane >= DX)
    def _():
        ring[plane & 7] = jnp.zeros_like(ring[0])


def stencil_kernel(x0, x1, first, v_ref, matrix_ref, *rest):
    out_ref, ring = rest[-2:]
    plane = first + pl.program_id(0)
    clear_outside(ring, first, plane)

    @pl.when(plane < DX)
    def _():
        ring[plane & 7] = v_ref[0]

    x = plane - 2

    @pl.when(x >= x0)
    def _():
        for _, rows, total, rest_of_it in sweep_pieces(ring, matrix_ref, x):
            out_ref[0, rows] = (total + rest_of_it.astype(jnp.float32)).astype(jnp.bfloat16)


def whole(shape):
    return pl.BlockSpec(shape, lambda i: (0,) * len(shape))


def settings(moved=0):
    return dict(
        compiler_params=pltpu.CompilerParams(
            vmem_limit_bytes=VMEM_BYTES, dimension_semantics=("arbitrary",)
        ),
        cost_estimate=pl.CostEstimate(flops=0, bytes_accessed=moved, transcendentals=0),
    )


def stencil_chunk(x0, x1, bands, matrix, so_far):
    first = max(0, x0 - 2)
    in_specs = [
        pl.BlockSpec((1, PLANE, NB), lambda i: (jnp.minimum(first + i, DX - 1), 0, 0)),
        whole((384, ROWS)),
    ]
    args = [bands, matrix]
    aliases = {}
    if so_far is not None:
        in_specs.append(pl.BlockSpec(memory_space=pl.ANY))
        args.append(so_far)
        aliases = {2: 0}
    return pl.pallas_call(
        functools.partial(stencil_kernel, x0, x1, first),
        grid=(x1 + 2 - first,),
        in_specs=in_specs,
        out_specs=pl.BlockSpec((1, PLANE, NB), lambda i: (jnp.maximum(first + i - 2, x0), 0, 0)),
        out_shape=jax.ShapeDtypeStruct((DX, PLANE, NB), jnp.bfloat16),
        scratch_shapes=[pltpu.VMEM((RING, PLANE, NB), jnp.bfloat16)],
        input_output_aliases=aliases,
        name=f"stencil_{x0}",
        **settings(),
    )(*args)


def sweep_kernel(
    x0, x1, first, parts,
    v_ref, once_ref, below_ref, own_ref, above_ref, occ_ref, support_ref, matrix_ref,
    *rest,
):
    swept_ref, dens_ref = rest[:2]
    send_refs = rest[2 : 2 + len(parts)]
    ring, pot_ring, pot_cells, turn, leaving = rest[2 + len(parts) :]
    step = pl.program_id(0)
    plane = first + step
    clear_outside(ring, first, plane)

    @pl.when(step == 0)
    def _():
        turn[...] = jnp.zeros_like(turn)
        for ref, low, high, at in ((below_ref, 8, 16, 0), (own_ref, 0, 16, 8), (above_ref, 0, 8, 24)):
            turn[0:72] = ref[0:72] * POT
            turned = turn[...].T
            for y in range(YB):
                pot_cells[DZ * y + at : DZ * y + at + high - low] = turned[CZ * y + low : CZ * y + high]

    @pl.when(plane < DX)
    def _():
        cells = pot_cells[...].astype(jnp.bfloat16)
        lines = lax.broadcasted_iota(jnp.int32, (128, 3 * 128), 0)
        blocks = lax.broadcasted_iota(jnp.int32, (128, 3 * 128), 1) >> 7
        chosen = jnp.where(lines == blocks * DX + plane, 1.0, 0.0).astype(jnp.bfloat16)
        spread = jnp.dot(cells, chosen, preferred_element_type=jnp.float32).astype(jnp.bfloat16)
        for block in range(3):
            rows = slice(ROWS * block, ROWS * block + ROWS)
            pot = spread[:, 128 * block : 128 * block + 128]
            pot_ring[plane & 7, rows] = pot
            ring[plane & 7, rows] = once_ref[0, rows] + jnp.concatenate([pot, pot], axis=1) * v_ref[0, rows]

    x = plane - 2

    @pl.when(x >= x0)
    def _():
        for piece, rows, total, rest_of_it in sweep_pieces(ring, matrix_ref, x):
            pot = pot_ring[x & 7, rows]
            rest_of_it = rest_of_it + jnp.concatenate([pot, pot], axis=1) * ring[x & 7, rows]
            total = (total + rest_of_it.astype(jnp.float32)) * (SCALE * SCALE)
            swept_ref[0, rows] = total.astype(jnp.bfloat16)
            down = total.reshape(2, DZ, NB)[:, 2 * B : 2 * B + DRIFT].reshape(2 * DRIFT, NB)
            leaving[16 * piece : 16 * piece + 16] = down.astype(jnp.bfloat16)
        for send_ref, (low, high) in zip(send_refs, parts):

            @pl.when(jnp.logical_and(x >= low, x < high))
            def _(send_ref=send_ref):
                send_ref[0] = leaving[...]

        occ = occ_ref[...]
        coarse = occ.astype(jnp.bfloat16).astype(jnp.float32)
        line = lax.broadcasted_iota(jnp.int32, (16, NB), 0)
        weights = jnp.where(line == 0, coarse, jnp.where(line == 1, occ - coarse, 0.0)).astype(jnp.bfloat16)
        cells = swept_ref[0]
        sums = lax.dot_general(
            weights, cells * cells, (((1,), (1,)), ((), ())), preferred_element_type=jnp.float32
        )
        dens_ref[pl.ds(x - x0, 1), :] = (sums[0:1] + sums[1:2]) * support_ref[pl.ds(x, 1), :]


def sweep_chunk(parts, bands, once, pots, occ, support, matrix):
    x0, x1 = parts[0][0], parts[-1][1]
    first = max(0, x0 - 2)
    in_plane = lambda i: (jnp.minimum(first + i, DX - 1), 0, 0)
    out_plane = lambda low, high: (lambda i: (jnp.clip(first + i - 2, low, high - 1) - low, 0, 0))
    planes = x1 - x0
    out = pl.pallas_call(
        functools.partial(sweep_kernel, x0, x1, first, parts),
        grid=(x1 + 2 - first,),
        in_specs=[
            pl.BlockSpec((1, PLANE, NB), in_plane),
            pl.BlockSpec((1, PLANE, NB), in_plane),
            whole((72, 128)),
            whole((72, 128)),
            whole((80, 128)),
            whole((1, NB)),
            whole((DX, PLANE)),
            whole((384, ROWS)),
        ],
        out_specs=[
            pl.BlockSpec((1, PLANE, NB), out_plane(x0, x1)),
            whole((planes, PLANE)),
        ]
        + [pl.BlockSpec((1, DX * DRIFT, NB), out_plane(low, high)) for low, high in parts],
        out_shape=[
            jax.ShapeDtypeStruct((planes, PLANE, NB), jnp.bfloat16),
            jax.ShapeDtypeStruct((planes, PLANE), jnp.float32),
        ]
        + [jax.ShapeDtypeStruct((high - low, DX * DRIFT, NB), jnp.bfloat16) for low, high in parts],
        scratch_shapes=[
            pltpu.VMEM((RING, PLANE, NB), jnp.bfloat16),
            pltpu.VMEM((RING, PLANE, 128), jnp.bfloat16),
            pltpu.VMEM((ROWS, 128), jnp.float32),
            pltpu.VMEM((128, 128), jnp.float32),
            pltpu.VMEM((DX * DRIFT, NB), jnp.bfloat16),
        ],
        name=f"sweeps_{x0}",
        **settings(planes * 10 * PLANE * NB if x0 else 0),
    )(bands, once, *pots, occ, support, matrix)
    return out[0], out[1], out[2:]


def recut_tables():
    line_y, line = np.divmod(np.arange(YR * DZCAP), DZCAP)
    own_y, own_z = np.divmod(np.arange(YR * DZ), DZ)
    next_y, next_z = np.divmod(np.arange(YR * DRIFT), DRIFT)
    y = np.concatenate([own_y, next_y])
    z = np.concatenate([own_z, next_z + DZ])
    shift = np.where(line_y[:, None] == y[None, :], z[None, :] - line[:, None], -1000)
    return shift.astype(np.int32), np.broadcast_to(z[None, :], (8, z.size)).astype(np.int32)


def recut_kernel(cuts_ref, shift_ref, source_ref, swept_ref, next_ref, *rest):
    out_ref, matrix = rest[-2:]

    @pl.when(pl.program_id(0) == 0)
    def _():
        c = lax.axis_index("gz")
        start_row = cuts_ref[c] - c * CZ
        last_row = cuts_ref[c + 1] - c * CZ + 2 * B
        chosen = jnp.logical_and(shift_ref[...] == start_row, source_ref[0:1] < last_row)
        matrix[...] = jnp.where(chosen, 1.0, 0.0).astype(jnp.bfloat16)

    columns = [
        jnp.concatenate(
            [swept_ref[0, YR * DZ * k : YR * DZ * (k + 1)], next_ref[0, YR * DRIFT * k : YR * DRIFT * (k + 1)]],
            axis=0,
        )
        for k in range(DX // YR)
    ]
    window = jnp.dot(matrix[...], jnp.concatenate(columns, axis=1), preferred_element_type=jnp.float32)
    for k in range(DX // YR):
        rows = window[:, NB * k : NB * k + NB].reshape(YR, DZCAP, NB)
        out_ref[0, YR * k : YR * k + YR] = rows.astype(jnp.bfloat16)


def recut(swept, x0, low, high, next_rows, z_cuts, so_far):
    shift, source = recut_tables()
    in_specs = [
        pl.BlockSpec(memory_space=pltpu.SMEM),
        whole(shift.shape),
        whole(source.shape),
        pl.BlockSpec((1, PLANE, NB), lambda i: (i + low - x0, 0, 0)),
        pl.BlockSpec((1, DX * DRIFT, NB), lambda i: (i, 0, 0)),
    ]
    args = [z_cuts, jnp.asarray(shift), jnp.asarray(source), swept, next_rows]
    aliases = {}
    if so_far is not None:
        in_specs.append(pl.BlockSpec(memory_space=pl.ANY))
        args.append(so_far)
        aliases = {5: 0}
    return pl.pallas_call(
        recut_kernel,
        grid=(high - low,),
        in_specs=in_specs,
        out_specs=pl.BlockSpec((1, DX, DZCAP, NB), lambda i: (i + low, 0, 0, 0)),
        out_shape=jax.ShapeDtypeStruct((DX, DX, DZCAP, NB), jnp.bfloat16),
        scratch_shapes=[pltpu.VMEM(shift.shape, jnp.bfloat16)],
        input_output_aliases=aliases,
        name=f"recut_{low}",
        **settings(),
    )(*args)


def both_sides(low, high, axis):
    size = lax.axis_size(axis)
    up = [(i, (i + 1) % size) for i in range(size)]
    down = [(j, i) for i, j in up]
    return lax.ppermute(low, axis, down), lax.ppermute(high, axis, up)


def from_behind(shard, axis, by):
    size = lax.axis_size(axis)
    pairs = [(i, i + by) for i in range(size) if 0 <= i + by < size]
    return lax.ppermute(shard, axis, pairs)


def atoms_kernel(cuts_ref, own_ref, arrivals_ref, atoms_ref, cells_ref):
    c = lax.axis_index("gz")
    slots = own_ref.shape[1]
    state = jnp.concatenate([own_ref[...], arrivals_ref[...]], axis=1)
    cells = state[COMP : COMP + 1] - 1.0
    lane = lax.broadcasted_iota(jnp.int32, (1, 2 * slots), 1)
    here = cells >= cuts_ref[c].astype(jnp.float32)
    comes = jnp.logical_and(cells < cuts_ref[c + 1].astype(jnp.float32), c + 1 < lax.axis_size("gz"))
    taken = jnp.where(lane < slots, jnp.where(here, 1.0, 0.0), jnp.where(comes, 1.0, 0.0))
    column = jnp.broadcast_to(taken, (128, 2 * slots)).T
    source = lax.broadcasted_iota(jnp.int32, (2 * slots, 2 * slots), 0)
    target = lax.broadcasted_iota(jnp.int32, (2 * slots, 2 * slots), 1)
    before = jnp.where(target <= source, 1.0, 0.0).astype(jnp.bfloat16)
    count = jnp.dot(before, column.astype(jnp.bfloat16), preferred_element_type=jnp.float32)
    count = jnp.concatenate([count, count], axis=1)
    column = jnp.concatenate([column, column], axis=1)
    chosen = jnp.logical_and(column > 0.5, count - 1.0 == target.astype(jnp.float32))
    table = jnp.where(chosen, 1.0, 0.0).astype(jnp.bfloat16)
    high = state.astype(jnp.bfloat16).astype(jnp.float32)
    middle = (state - high).astype(jnp.bfloat16).astype(jnp.float32)
    parts = jnp.concatenate([high, middle, state - high - middle, jnp.zeros_like(high)], axis=0)
    placed = jnp.dot(parts.astype(jnp.bfloat16), table, preferred_element_type=jnp.float32)
    placed = placed[0:8] + placed[8:16] + placed[16:24]
    atoms_ref[...] = placed[0:COMP]
    cells_ref[...] = placed[COMP : COMP + 1].astype(jnp.int32) - 1


def place_atoms(z_cuts, own, arrivals):
    vmem = pl.BlockSpec(memory_space=pltpu.VMEM)
    atoms, cells = pl.pallas_call(
        atoms_kernel,
        in_specs=[pl.BlockSpec(memory_space=pltpu.SMEM), vmem, vmem],
        out_specs=[vmem, vmem],
        out_shape=[
            jax.ShapeDtypeStruct((COMP, ACAP), jnp.float32),
            jax.ShapeDtypeStruct((1, ACAP), jnp.int32),
        ],
        name="atoms",
    )(z_cuts, own, arrivals)
    return atoms, cells.reshape(ACAP)


def local(wave_bands, potential, occupation, support, z_cuts, atom_state, atom_cell):
    bands = wave_bands.reshape(DX, PLANE, NB)
    occ = occupation.reshape(1, NB)
    weights = support.reshape(DX, PLANE)
    matrix = jnp.asarray(stencil_matrix())

    pots = potential.reshape(CX, YB * CZ)
    once = None
    for axis, (x0, x1) in zip(("gx", "gy"), ((0, 8), (8, 16))):
        after, before = both_sides(pots, pots, axis)
        once = stencil_chunk(x0, x1, bands, matrix, once)
        pots = jnp.concatenate([before, pots, after], axis=0)
        pots, once = lax.optimization_barrier((pots, once))
    atoms = jnp.concatenate(
        [atom_state, (atom_cell + 1).astype(jnp.float32)[None, :], jnp.zeros((3, atom_cell.size), jnp.float32)],
        axis=0,
    )
    after, before = both_sides(jnp.concatenate([pots, atoms], axis=0), pots, "gz")
    once = stencil_chunk(16, 24, bands, matrix, once)
    arriving_atoms = after[72:]
    pots = (before, pots, after)

    swept, dens, arrivals = [], [], []
    new_bands = None
    for index, parts in enumerate(CHUNKS):
        if index == 2:
            new_bands = recut(swept[0], 0, *CHUNKS[0][0], arrivals[0][0], z_cuts, None)
            occ, new_bands = lax.optimization_barrier((occ, new_bands))
        chunk, chunk_dens, sends = sweep_chunk(parts, bands, once, pots, occ, weights, matrix)
        swept.append(chunk)
        occ, chunk_dens = lax.optimization_barrier((occ, chunk_dens))
        dens.append(chunk_dens)
        arrivals.append([from_behind(send, "gz", -1) for send in sends])

    pieces = [
        (index, parts[0][0], low, high, arrival)
        for index, parts in enumerate(CHUNKS)
        for arrival, (low, high) in zip(arrivals[index], parts)
    ][1:]

    def recut_next(new_bands):
        index, x0, low, high, arrival = pieces.pop(0)
        return recut(swept[index], x0, low, high, arrival, z_cuts, new_bands)

    low_side = jnp.concatenate([dens[0], dens[1][:4]], axis=0)
    from_above, from_below = both_sides(low_side, dens[2][4:], "gx")
    inside = jnp.concatenate([dens[1][4:], dens[2][:4]], axis=0)
    new_bands = recut_next(recut_next(new_bands))
    from_above, from_below, new_bands = lax.optimization_barrier((from_above, from_below, new_bands))
    dens = inside + from_above + from_below
    from_above, from_below = both_sides(dens[:, :ROWS], dens[:, 2 * ROWS :], "gy")
    dens = dens[:, ROWS : 2 * ROWS] + from_above + from_below
    while len(pieces) > 1:
        new_bands = recut_next(new_bands)
    dens, new_bands = lax.optimization_barrier((dens, new_bands))
    from_above, from_below = both_sides(dens, dens, "gz")
    shape = (CX, YB, DZ)
    inside = dens.reshape(shape)[:, :, B : B + CZ]
    lower = from_below.reshape(shape)[:, :, B + CZ :]
    upper = from_above.reshape(shape)[:, :, :B]
    density = inside + jnp.concatenate([lower, upper], axis=2)
    new_bands = recut_next(new_bands)

    new_atoms, new_cells = place_atoms(z_cuts, atoms, arriving_atoms)
    return (density, new_bands, new_atoms, new_cells)


def solution(mesh):
    in_specs = (
        P("gx", "gy", "gz", None),
        P("gx", "gy", "gz"),
        P("gx", "gy", "gz", None),
        P("gx", "gy", "gz"),
        P(),
        P(None, ("gx", "gy", "gz")),
        P(("gx", "gy", "gz")),
    )
    out_specs = (
        P("gx", "gy", "gz"),
        P("gx", "gy", "gz", None),
        P(None, ("gx", "gy", "gz")),
        P(("gx", "gy", "gz")),
    )
    return jax.shard_map(local, mesh=mesh, in_specs=in_specs, out_specs=out_specs, check_vma=False)
```

time: 361 us -> 138 us (0.38)
  other arithmetic: 239 us -> 1.37 us
  Pallas kernels: 0 us -> 83.1 us
  waiting for transfers between devices: 85 us -> 4.9 us
  starting transfers between devices: 25.6 us -> 41.4 us
    convert_element_type x6 -> x0, other arithmetic: 114 us -> none  [the longest x2 113 us: relax_sweep(): values = wave_set.astype(jnp.float32)]
    reduce_sum x3 -> x0, other arithmetic: 107 us -> none  [the longest x1 107 us: local(): domain_density = support * jnp.sum(values * values * band_weights, axis=-1)]
    pallas_call x0 -> x13, Pallas kernels: none -> 83.1 us  [the longest x3 35.9 us: sweep_chunk(): pl.pallas_call(functools.partial(sweep_kernel, x0, x1, first, parts), gri...]
    ppermute x12, waiting for transfers between devices: 85 us -> 4.88 us  [both_sides(): return (lax.ppermute(low, axis, down), lax.ppermute(high, axis, up))]
    ppermute x2 -> x6, starting transfers between devices: 5.38 us -> 21.3 us  [from_behind(): return lax.ppermute(shard, axis, pairs)]
    select_n x3 -> x0, other arithmetic: 13.1 us -> none  [the longest x1 13.1 us: local(): jnp.where(keep_rows[None, None, :, None], window, jnp.zeros((), jnp.bfloa...]
  transfers between devices with their start and end apart: 14 -> 18, of which waited for: 9 -> 2; matrix products, arithmetic and copies ran while one was open for 6% -> 1% of each run, Pallas kernels for 0% -> 56%
where the time goes in v1:
time: 138 us; the launch traced here: 137 us
  Pallas kernels  83.1 us (60%)
  starting transfers between devices  41.4 us (30%)
  local copies, waits for them, and re-layouts  5.18 us (4%)
  waiting for transfers between devices  4.9 us (4%)
    pallas_call x3, Pallas kernels, sweep_chunk(): pl.pallas_call(functools.partial(sweep_kernel, x0, x1, first, parts), gri...  35.9 us
    pallas_call x3, Pallas kernels, stencil_chunk(): pl.pallas_call(functools.partial(stencil_kernel, x0, x1, first), grid=(x1...  27 us
    ppermute x6, starting transfers between devices, from_behind(): return lax.ppermute(shard, axis, pairs)  21.3 us
    ppermute x12, starting transfers between devices, both_sides(): return (lax.ppermute(low, axis, down), lax.ppermute(high, axis, up))  20.1 us
    pallas_call x6, Pallas kernels, recut(): pl.pallas_call(recut_kernel, grid=(high - low,), in_specs=in_specs, out_s...  18.5 us
    ppermute x12, waiting for transfers between devices, both_sides(): return (lax.ppermute(low, axis, down), lax.ppermute(high, axis, up))  4.88 us
    unnamed x26, local copies, waits for them, and re-layouts  3.32 us
  transfers between devices with their start and end apart: 18, of which 2 were waited for; matrix products, arithmetic and copies ran while one was open for 1% of the time, Pallas kernels for 56%

profile of v1, /device:TPU:22, one launch (start us, length us, event | category | flops | bytes accessed | tf_op | source)
XLA Modules:
  0.0 136.9 jit_solution(15451012895043502420)
XLA Ops:
  0.6 0.8 reshape.34
  1.5 0.7 collective-permute-start.1
  2.2 0.0 collective-permute-start
  2.2 0.9 copy-done.2
  3.1 8.4 %stencil_0.1.rest_0_ = bf16[24,768,256]{2,1,0:T(8,128)(2,1)} custom-call(bf16[24,768,256]{2,1,0:T(8,128)(2,1)} %bitcast.11, bf16[384,256]{1,0:T(8,128)(2,1)S(1)} %copy-done.2), custom_call_target="tpu_custom_call" | custom-call | tf_op jit(solution)/shard_map/stencil_0/pallas_call | solution.py:134
  11.5 0.0 collective-permute-done.1
  11.6 0.0 collective-permute-done
  11.6 4.1 %collective-permute-start.3 = (f32[24,128]{1,0:T(8,128)S(1)}, f32[24,128]{1,0:T(8,128)S(1)}, u32[]{:S(2)}, u32[]{:S(2)}) collective-permute-start(f32[24,128]{1,0:T(8,128)S(1)} %pad_maximum_fusion.3), channel_id=1, source_target_pairs={{8,0},{16,8},{24,16},{0,24},{9,1},{17,9},{25,17},{1,25},{10,2},{18... | collective-permute-start | bytes 36872 | tf_op jit(solution)/shard_map/ppermute | solution.py:317
  15.6 0.0 collective-permute-start.2
  15.7 0.0 copy-start.9
  15.7 0.0 copy-start.8
  15.7 0.0 copy-start.3
  15.7 9.5 %stencil_8.1.rest_0_ = bf16[24,768,256]{2,1,0:T(8,128)(2,1)} custom-call(bf16[24,768,256]{2,1,0:T(8,128)(2,1)} %bitcast.12, bf16[384,256]{1,0:T(8,128)(2,1)S(1)} %copy-done.2, bf16[24,768,256]{2,1,0:T(8,128)(2,1)} %stencil_0.1.rest_0_), custom_call_target="tpu_custom_call", output_to_operand_aliasing={{}: (2, {})} | custom-call | tf_op jit(solution)/shard_map/stencil_8/pallas_call | solution.py:134
  25.2 0.0 collective-permute-done.3
  25.2 0.0 collective-permute-done.2
  25.3 0.7 collective-permute-start.5
  26.0 5.0 %collective-permute-start.4 = (f32[72,128]{1,0:T(8,128)S(1)}, f32[72,128]{1,0:T(8,128)S(1)}, u32[]{:S(2)}, u32[]{:S(2)}) collective-permute-start(f32[72,128]{1,0:T(8,128)S(1)} %pad_maximum_fusion.1.own_ref), channel_id=1, source_target_pairs={{0,1},{1,2},{2,3},{3,4},{4,5},{5,6},{6,7},{7,0},{8,9},{9,10},{10,1... | collective-permute-start | bytes 110600 | tf_op jit(solution)/shard_map/ppermute | solution.py:317
  31.0 0.1 reshape.35.support_ref
  31.1 0.0 copy-start.7
  31.1 9.1 %stencil_16.1.once_ref = bf16[24,768,256]{2,1,0:T(8,128)(2,1)} custom-call(bf16[24,768,256]{2,1,0:T(8,128)(2,1)} %bitcast.13, bf16[384,256]{1,0:T(8,128)(2,1)S(1)} %copy-done.3, bf16[24,768,256]{2,1,0:T(8,128)(2,1)} %stencil_8.1.rest_0_), custom_call_target="tpu_custom_call", output_to_operand_aliasing={{}: (2, {})} | custom-call | tf_op jit(solution)/shard_map/stencil_16/pallas_call | solution.py:134
  40.2 0.0 collective-permute-done.4.below_ref
  40.2 0.0 collective-permute-done.5.above_ref
  40.2 6.6 %sweeps_0.1 = (bf16[4,768,256]{2,1,0:T(8,128)(2,1)S(1)}, f32[4,768]{1,0:T(4,128)S(1)}, bf16[4,192,256]{2,1,0:T(8,128)(2,1)S(1)}) custom-call(bf16[24,768,256]{2,1,0:T(8,128)(2,1)} %bitcast.14, bf16[24,768,256]{2,1,0:T(8,128)(2,1)} %stencil_16.1.once_ref, f32[72,128]{1,0:T(8,128)S(1)} %collective-permute-done.4.below_ref, ...), custom_call_target="tpu_custom_call" | custom-call | tf_op jit(solution)/shard_map/sweeps_0/pallas_call | solution.py:215
  46.8 1.3 collective-permute-start.6
  48.2 0.0 copy-start.1
  48.2 0.0 copy-start.4
  48.2 0.0 copy-start.5
  48.2 12.2 %sweeps_4.1 = (bf16[8,768,256]{2,1,0:T(8,128)(2,1)S(1)}, f32[8,768]{1,0:T(8,128)S(1)}, bf16[4,192,256]{2,1,0:T(8,128)(2,1)S(1)}, bf16[4,192,256]{2,1,0:T(8,128)(2,1)S(1)}) custom-call(bf16[24,768,256]{2,1,0:T(8,128)(2,1)} %bitcast.15, bf16[24,768,256]{2,1,0:T(8,128)(2,1)} %stencil_16.1.once_ref, f32[72,128]{1,0:T(8,128)S(1)} %collective-permute-done.4.below_ref, ...), custom_call_target="tpu_custom_call" | custom-call | bytes 15728640 | tf_op jit(solution)/shard_map/sweeps_4/pallas_call | solution.py:215
  60.4 5.1 %collective-permute-start.10 = (bf16[4,192,256]{2,1,0:T(8,128)(2,1)S(1)}, bf16[4,192,256]{2,1,0:T(8,128)(2,1)S(1)}, u32[]{:S(2)}, u32[]{:S(2)}) collective-permute-start(bf16[4,192,256]{2,1,0:T(8,128)(2,1)S(1)} %get-tuple-element.51), channel_id=1, source_target_pairs={{1,0},{2,1},{3,2},{4,3},{5,4},{6,5},{7,6},{9,8},{10,9},{11,10},{12... | collective-permute-start | bytes 1179656 | tf_op jit(solution)/shard_map/ppermute | solution.py:323
  65.5 1.9 %collective-permute-start.9 = (bf16[4,192,256]{2,1,0:T(8,128)(2,1)S(1)}, bf16[4,192,256]{2,1,0:T(8,128)(2,1)S(1)}, u32[]{:S(2)}, u32[]{:S(2)}) collective-permute-start(bf16[4,192,256]{2,1,0:T(8,128)(2,1)S(1)} %get-tuple-element.50), channel_id=1, source_target_pairs={{1,0},{2,1},{3,2},{4,3},{5,4},{6,5},{7,6},{9,8},{10,9},{11,10},{12... | collective-permute-start | bytes 1179656 | tf_op jit(solution)/shard_map/ppermute | solution.py:323
  67.5 0.5 collective-permute-start.7
  67.9 0.0 collective-permute-done.6.next_ref
  68.0 3.1 %recut_0.1.rest_0_ = bf16[24,24,40,256]{3,2,1,0:T(8,128)(2,1)} custom-call(s32[9]{0:T(128)S(1)} %copy-done.5, s32[240,240]{1,0:T(8,128)S(1)} %copy-done.1, s32[8,240]{1,0:T(8,128)S(1)} %copy-done.4, bf16[4,768,256]{2,1,0:T(8,128)(2,1)S(1)} %get-tuple-element.43.swept_ref, bf16[4,192,256]{2,1,0:T(8,128)(2,1)S(1)} %collective-permute-done.6.next_ref), custom_call_target="tpu_custom_call" | custom-call | tf_op jit(solution)/shard_map/recut_0/pallas_call | solution.py:300
  71.0 17.2 %sweeps_12.1 = (bf16[12,768,256]{2,1,0:T(8,128)(2,1)}, f32[12,768]{1,0:T(8,128)S(1)}, bf16[4,192,256]{2,1,0:T(8,128)(2,1)S(1)}, bf16[4,192,256]{2,1,0:T(8,128)(2,1)S(1)}, bf16[4,192,256]{2,1,0:T(8,128)(2,1)S(1)}) custom-call(bf16[24,768,256]{2,1,0:T(8,128)(2,1)} %bitcast.16, bf16[24,768,256]{2,1,0:T(8,128)(2,1)} %stencil_16.1.once_ref, ...), custom_call_target="tpu_custom_call" | custom-call | bytes 23592960 | tf_op jit(solution)/shard_map/sweeps_12/pallas_call | solution.py:215
  88.2 0.2 collective-permute-start.8
  88.4 5.4 %collective-permute-start.13 = (bf16[4,192,256]{2,1,0:T(8,128)(2,1)S(1)}, bf16[4,192,256]{2,1,0:T(8,128)(2,1)S(1)}, u32[]{:S(2)}, u32[]{:S(2)}) collective-permute-start(bf16[4,192,256]{2,1,0:T(8,128)(2,1)S(1)} %get-tuple-element.56), channel_id=1, source_target_pairs={{1,0},{2,1},{3,2},{4,3},{5,4},{6,5},{7,6},{9,8},{10,9},{11,10},{12... | collective-permute-start | bytes 1179656 | tf_op jit(solution)/shard_map/ppermute | solution.py:323
  93.8 0.0 collective-permute-done.10.next_ref
  93.8 1.9 %collective-permute-start.14 = (bf16[4,192,256]{2,1,0:T(8,128)(2,1)S(1)}, bf16[4,192,256]{2,1,0:T(8,128)(2,1)S(1)}, u32[]{:S(2)}, u32[]{:S(2)}) collective-permute-start(bf16[4,192,256]{2,1,0:T(8,128)(2,1)S(1)} %get-tuple-element.57), channel_id=1, source_target_pairs={{1,0},{2,1},{3,2},{4,3},{5,4},{6,5},{7,6},{9,8},{10,9},{11,10},{12... | collective-permute-start | bytes 1179656 | tf_op jit(solution)/shard_map/ppermute | solution.py:323
  95.7 3.1 %recut_4.1.rest_0_ = bf16[24,24,40,256]{3,2,1,0:T(8,128)(2,1)} custom-call(s32[9]{0:T(128)S(1)} %copy-done.5, s32[240,240]{1,0:T(8,128)S(1)} %copy-done.1, s32[8,240]{1,0:T(8,128)S(1)} %copy-done.4, bf16[8,768,256]{2,1,0:T(8,128)(2,1)S(1)} %get-tuple-element.49.swept_ref, ...), custom_call_target="tpu_custom_call", output_to_operand_aliasing={{}: (5, {})} | custom-call | tf_op jit(solution)/shard_map/recut_4/pallas_call | solution.py:300
  98.8 0.0 collective-permute-done.9.next_ref
  98.8 5.6 %collective-permute-start.17 = (bf16[4,192,256]{2,1,0:T(8,128)(2,1)S(1)}, bf16[4,192,256]{2,1,0:T(8,128)(2,1)S(1)}, u32[]{:S(2)}, u32[]{:S(2)}) collective-permute-start(bf16[4,192,256]{2,1,0:T(8,128)(2,1)S(1)} %get-tuple-element.60), channel_id=1, source_target_pairs={{1,0},{2,1},{3,2},{4,3},{5,4},{6,5},{7,6},{9,8},{10,9},{11,10},{12... | collective-permute-start | bytes 1179656 | tf_op jit(solution)/shard_map/ppermute | solution.py:323
  104.5 3.1 %recut_8.1.rest_0_ = bf16[24,24,40,256]{3,2,1,0:T(8,128)(2,1)} custom-call(s32[9]{0:T(128)S(1)} %copy-done.5, s32[240,240]{1,0:T(8,128)S(1)} %copy-done.1, s32[8,240]{1,0:T(8,128)S(1)} %copy-done.4, bf16[8,768,256]{2,1,0:T(8,128)(2,1)S(1)} %get-tuple-element.49.swept_ref, ...), custom_call_target="tpu_custom_call", output_to_operand_aliasing={{}: (5, {})} | custom-call | tf_op jit(solution)/shard_map/recut_8/pallas_call | solution.py:300
  107.6 0.0 collective-permute-done.7
  107.6 0.0 collective-permute-done.8
  107.6 3.3 %collective-permute-start.11 = (f32[8,256]{1,0:T(8,128)S(1)}, f32[8,256]{1,0:T(8,128)S(1)}, u32[]{:S(2)}, u32[]{:S(2)}) collective-permute-start(f32[8,256]{1,0:T(8,128)S(1)} %get-tuple-element.64), channel_id=1, source_target_pairs={{8,0},{16,8},{24,16},{0,24},{9,1},{17,9},{25,17},{1,25},{10,2},{18... | collective-permute-start | bytes 24584 | tf_op jit(solution)/shard_map/ppermute | solution.py:317
  110.9 0.0 collective-permute-start.12
  110.9 1.4 collective-permute-done.11
  112.3 3.5 %collective-permute-done.12 = f32[8,256]{1,0:T(8,128)S(1)} collective-permute-done((f32[8,256]{1,0:T(8,128)S(1)}, f32[8,256]{1,0:T(8,128)S(1)}, u32[]{:S(2)}, u32[]{:S(2)}) %collective-permute-start.12) | collective-permute-done | bytes 8224 | tf_op jit(solution)/shard_map/ppermute | solution.py:317
  115.8 0.0 collective-permute-done.14.next_ref
  115.8 3.1 %recut_12.1.rest_0_ = bf16[24,24,40,256]{3,2,1,0:T(8,128)(2,1)} custom-call(s32[9]{0:T(128)S(1)} %copy-done.5, s32[240,240]{1,0:T(8,128)S(1)} %copy-done.1, s32[8,240]{1,0:T(8,128)S(1)} %copy-done.4, bf16[12,768,256]{2,1,0:T(8,128)(2,1)S(1)} %bitcast.7, bf16[4,192,256]{2,1,0:T(8,128)(2,1)S(1)} %collective-permute-done.14.next_ref, ...), custom_call_target="tpu_custom_call", output_to_operand_aliasing={{}: (5, {})} | custom-call | tf_op jit(solution)/shard_map/recut_12/pallas_call | solution.py:300
  118.9 3.1 %recut_16.1.rest_0_ = bf16[24,24,40,256]{3,2,1,0:T(8,128)(2,1)} custom-call(s32[9]{0:T(128)S(1)} %copy-done.5, s32[240,240]{1,0:T(8,128)S(1)} %copy-done.1, s32[8,240]{1,0:T(8,128)S(1)} %copy-done.4, bf16[12,768,256]{2,1,0:T(8,128)(2,1)S(1)} %bitcast.7, bf16[4,192,256]{2,1,0:T(8,128)(2,1)S(1)} %collective-permute-done.13.next_ref, ...), custom_call_target="tpu_custom_call", output_to_operand_aliasing={{}: (5, {})} | custom-call | tf_op jit(solution)/shard_map/recut_16/pallas_call | solution.py:300
  122.0 1.3 collective-permute-start.16
  123.3 4.4 %collective-permute-start.15 = (f32[8,256]{1,0:T(8,128)S(1)}, f32[8,256]{1,0:T(8,128)S(1)}, u32[]{:S(2)}, u32[]{:S(2)}) collective-permute-start(f32[8,256]{1,0:T(8,128)S(1)} %fusion.1), channel_id=1, source_target_pairs={{0,1},{1,2},{2,3},{3,4},{4,5},{5,6},{6,7},{7,0},{8,9},{9,10},{10,1... | collective-permute-start | bytes 24584 | tf_op jit(solution)/shard_map/ppermute | solution.py:317
  127.6 0.6 pad_maximum_fusion.4.own_ref
  128.2 0.6 slice.50.arrivals_ref
  128.8 1.7 %atoms.1 = (f32[4,256]{1,0:T(4,128)}, s32[1,256]{1,0:T(1,128)}) custom-call(s32[9]{0:T(128)} %cuts_ref.13, f32[8,128]{1,0:T(8,128)} %pad_maximum_fusion.4.own_ref, f32[8,128]{1,0:T(8,128)} %slice.50.arrivals_ref), custom_call_target="tpu_custom_call" | custom-call | tf_op jit(solution)/shard_map/atoms/pallas_call | solution.py:355
  130.5 0.1 reshape.36
  130.6 2.3 %copy-done = bf16[12,768,256]{2,1,0:T(8,128)(2,1)S(1)} copy-done((bf16[12,768,256]{2,1,0:T(8,128)(2,1)S(1)}, bf16[12,768,256]{2,1,0:T(8,128)(2,1)}, u32[]{:S(2)}) %copy-start) | copy-done | bytes 4718616
  132.9 3.0 %recut_20.1 = bf16[24,24,40,256]{3,2,1,0:T(8,128)(2,1)} custom-call(s32[9]{0:T(128)S(1)} %copy-done.6, s32[240,240]{1,0:T(8,128)S(1)} %copy-done.1, s32[8,240]{1,0:T(8,128)S(1)} %copy-done.4, bf16[12,768,256]{2,1,0:T(8,128)(2,1)S(1)} %copy-done, bf16[4,192,256]{2,1,0:T(8,128)(2,1)S(1)} %collective-permute-done.17.next_ref, ...), custom_call_target="tpu_custom_call", output_to_operand_aliasing={{}: (5, {})} | custom-call | tf_op jit(solution)/shard_map/recut_20/pallas_call | solution.py:300
  136.0 0.1 reshape.37
  136.1 0.1 slice.48
  136.1 0.0 collective-permute-done.16
  136.2 0.1 reshape.38
  136.2 0.7 slice_add_fusion
  (33 shorter events, 0.1 us)
Async XLA Ops:
  1.5 10.1 %collective-permute-start.1 = (f32[8,128]{1,0:T(8,128)S(1)}, f32[8,128]{1,0:T(8,128)S(1)}, u32[]{:S(2)}, u32[]{:S(2)}) collective-permute-start(f32[8,128]{1,0:T(8,128)S(1)} %reshape.34), channel_id=1, source_target_pairs={{32,0},{64,32},{96,64},{0,96},{33,1},{65,33},{97,65},{1,97},{34,2}... | collective-permute-start | bytes 12296 | tf_op jit(solution)/shard_map/ppermute | solution.py:317
  2.2 9.4 %collective-permute-start = (f32[8,128]{1,0:T(8,128)S(1)}, f32[8,128]{1,0:T(8,128)S(1)}, u32[]{:S(2)}, u32[]{:S(2)}) collective-permute-start(f32[8,128]{1,0:T(8,128)S(1)} %reshape.34), channel_id=1, source_target_pairs={{0,32},{32,64},{64,96},{96,0},{1,33},{33,65},{65,97},{97,1},{2,34}... | collective-permute-start | bytes 12296 | tf_op jit(solution)/shard_map/ppermute | solution.py:317
  2.2 0.9 copy-start.2
  3.1 12.5 %copy-start.10 = (s32[128]{0:T(128)S(1)}, s32[128]{0:T(128)}, u32[]{:S(2)}) copy-start(s32[128]{0:T(128)} %param.26) | copy-start | bytes 1540
  11.6 13.7 %collective-permute-start.3 = (f32[24,128]{1,0:T(8,128)S(1)}, f32[24,128]{1,0:T(8,128)S(1)}, u32[]{:S(2)}, u32[]{:S(2)}) collective-permute-start(f32[24,128]{1,0:T(8,128)S(1)} %pad_maximum_fusion.3), channel_id=1, source_target_pairs={{8,0},{16,8},{24,16},{0,24},{9,1},{17,9},{25,17},{1,25},{10,2},{18... | collective-permute-start | bytes 36872 | tf_op jit(solution)/shard_map/ppermute | solution.py:317
  15.6 9.6 %collective-permute-start.2 = (f32[24,128]{1,0:T(8,128)S(1)}, f32[24,128]{1,0:T(8,128)S(1)}, u32[]{:S(2)}, u32[]{:S(2)}) collective-permute-start(f32[24,128]{1,0:T(8,128)S(1)} %pad_maximum_fusion.3), channel_id=1, source_target_pairs={{0,8},{8,16},{16,24},{24,0},{1,9},{9,17},{17,25},{25,1},{2,10},{10... | collective-permute-start | bytes 36872 | tf_op jit(solution)/shard_map/ppermute | solution.py:317
  15.7 9.6 %copy-start.9 = (f32[4,128]{1,0:T(4,128)S(1)}, f32[4,128]{1,0:T(4,128)}, u32[]{:S(2)}) copy-start(f32[4,128]{1,0:T(4,128)} %param.25) | copy-start | bytes 6148
  15.7 15.3 %copy-start.8 = (f32[24,24,32]{2,1,0:T(8,128)S(1)}, f32[24,24,32]{2,1,0:T(8,128)}, u32[]{:S(2)}) copy-start(f32[24,24,32]{2,1,0:T(8,128)} %param.23) | copy-start | bytes 221188
  15.7 15.4 %copy-start.3 = (bf16[384,256]{1,0:T(8,128)(2,1)S(1)}, bf16[384,256]{1,0:T(8,128)(2,1)}, u32[]{:S(2)}) copy-start(bf16[384,256]{1,0:T(8,128)(2,1)} %constant.10.clone.matrix_ref) | copy-start | bytes 589828
  25.3 15.0 %collective-permute-start.5 = (f32[80,128]{1,0:T(8,128)S(1)}, f32[80,128]{1,0:T(8,128)S(1)}, u32[]{:S(2)}, u32[]{:S(2)}) collective-permute-start(f32[80,128]{1,0:T(8,128)S(1)} %pad_maximum_fusion), channel_id=1, source_target_pairs={{1,0},{2,1},{3,2},{4,3},{5,4},{6,5},{7,6},{0,7},{9,8},{10,9},{11,1... | collective-permute-start | bytes 122888 | tf_op jit(solution)/shard_map/ppermute | solution.py:317
  26.0 14.2 %collective-permute-start.4 = (f32[72,128]{1,0:T(8,128)S(1)}, f32[72,128]{1,0:T(8,128)S(1)}, u32[]{:S(2)}, u32[]{:S(2)}) collective-permute-start(f32[72,128]{1,0:T(8,128)S(1)} %pad_maximum_fusion.1.own_ref), channel_id=1, source_target_pairs={{0,1},{1,2},{2,3},{3,4},{4,5},{5,6},{6,7},{7,0},{8,9},{9,10},{10,1... | collective-permute-start | bytes 110600 | tf_op jit(solution)/shard_map/ppermute | solution.py:317
  31.1 9.1 %copy-start.7 = (f32[1,1,1,256]{3,2,1,0:T(1,128)S(1)}, f32[1,1,1,256]{3,2,1,0:T(1,128)}, u32[]{:S(2)}) copy-start(f32[1,1,1,256]{3,2,1,0:T(1,128)} %param.22) | copy-start | bytes 3076
  46.8 21.1 %collective-permute-start.6 = (bf16[4,192,256]{2,1,0:T(8,128)(2,1)S(1)}, bf16[4,192,256]{2,1,0:T(8,128)(2,1)S(1)}, u32[]{:S(2)}, u32[]{:S(2)}) collective-permute-start(bf16[4,192,256]{2,1,0:T(8,128)(2,1)S(1)} %get-tuple-element.44), channel_id=1, source_target_pairs={{1,0},{2,1},{3,2},{4,3},{5,4},{6,5},{7,6},{9,8},{10,9},{11,10},{12... | collective-permute-start | bytes 1179656 | tf_op jit(solution)/shard_map/ppermute | solution.py:323
  48.2 19.8 %copy-start.1 = (s32[240,240]{1,0:T(8,128)S(1)}, s32[240,240]{1,0:T(8,128)}, u32[]{:S(2)}) copy-start(s32[240,240]{1,0:T(8,128)} %constant.11.clone.shift_ref) | copy-start | bytes 691204
  48.2 19.8 %copy-start.4 = (s32[8,240]{1,0:T(8,128)S(1)}, s32[8,240]{1,0:T(8,128)}, u32[]{:S(2)}) copy-start(s32[8,240]{1,0:T(8,128)} %constant.12.clone.source_ref) | copy-start | bytes 23044
  48.2 19.8 %copy-start.5 = (s32[9]{0:T(128)S(1)}, s32[9]{0:T(128)}, u32[]{:S(2)}) copy-start(s32[9]{0:T(128)} %cuts_ref.13) | copy-start | bytes 112
  60.4 33.4 %collective-permute-start.10 = (bf16[4,192,256]{2,1,0:T(8,128)(2,1)S(1)}, bf16[4,192,256]{2,1,0:T(8,128)(2,1)S(1)}, u32[]{:S(2)}, u32[]{:S(2)}) collective-permute-start(bf16[4,192,256]{2,1,0:T(8,128)(2,1)S(1)} %get-tuple-element.51), channel_id=1, source_target_pairs={{1,0},{2,1},{3,2},{4,3},{5,4},{6,5},{7,6},{9,8},{10,9},{11,10},{12... | collective-permute-start | bytes 1179656 | tf_op jit(solution)/shard_map/ppermute | solution.py:323
  65.5 33.3 %collective-permute-start.9 = (bf16[4,192,256]{2,1,0:T(8,128)(2,1)S(1)}, bf16[4,192,256]{2,1,0:T(8,128)(2,1)S(1)}, u32[]{:S(2)}, u32[]{:S(2)}) collective-permute-start(bf16[4,192,256]{2,1,0:T(8,128)(2,1)S(1)} %get-tuple-element.50), channel_id=1, source_target_pairs={{1,0},{2,1},{3,2},{4,3},{5,4},{6,5},{7,6},{9,8},{10,9},{11,10},{12... | collective-permute-start | bytes 1179656 | tf_op jit(solution)/shard_map/ppermute | solution.py:323
  67.5 40.1 %collective-permute-start.7 = (f32[8,768]{1,0:T(8,128)S(1)}, f32[8,768]{1,0:T(8,128)S(1)}, u32[]{:S(2)}, u32[]{:S(2)}) collective-permute-start(f32[8,768]{1,0:T(8,128)S(1)} %pad_maximum_fusion.2), channel_id=1, source_target_pairs={{32,0},{64,32},{96,64},{0,96},{33,1},{65,33},{97,65},{1,97},{34,2}... | collective-permute-start | bytes 73736 | tf_op jit(solution)/shard_map/ppermute | solution.py:317
  88.2 19.4 %collective-permute-start.8 = (f32[8,768]{1,0:T(8,128)S(1)}, f32[8,768]{1,0:T(8,128)S(1)}, u32[]{:S(2)}, u32[]{:S(2)}) collective-permute-start(f32[8,768]{1,0:T(8,128)S(1)} %slice.36), channel_id=1, source_target_pairs={{0,32},{32,64},{64,96},{96,0},{1,33},{33,65},{65,97},{97,1},{2,34}... | collective-permute-start | bytes 73736 | tf_op jit(solution)/shard_map/ppermute | solution.py:317
  88.4 30.5 %collective-permute-start.13 = (bf16[4,192,256]{2,1,0:T(8,128)(2,1)S(1)}, bf16[4,192,256]{2,1,0:T(8,128)(2,1)S(1)}, u32[]{:S(2)}, u32[]{:S(2)}) collective-permute-start(bf16[4,192,256]{2,1,0:T(8,128)(2,1)S(1)} %get-tuple-element.56), channel_id=1, source_target_pairs={{1,0},{2,1},{3,2},{4,3},{5,4},{6,5},{7,6},{9,8},{10,9},{11,10},{12... | collective-permute-start | bytes 1179656 | tf_op jit(solution)/shard_map/ppermute | solution.py:323
  93.8 22.0 %collective-permute-start.14 = (bf16[4,192,256]{2,1,0:T(8,128)(2,1)S(1)}, bf16[4,192,256]{2,1,0:T(8,128)(2,1)S(1)}, u32[]{:S(2)}, u32[]{:S(2)}) collective-permute-start(bf16[4,192,256]{2,1,0:T(8,128)(2,1)S(1)} %get-tuple-element.57), channel_id=1, source_target_pairs={{1,0},{2,1},{3,2},{4,3},{5,4},{6,5},{7,6},{9,8},{10,9},{11,10},{12... | collective-permute-start | bytes 1179656 | tf_op jit(solution)/shard_map/ppermute | solution.py:323
  98.8 17.0 %slice-start = ((s8[4718592]{0:T(1024)(128)(4,1)}), s8[4194304]{0:T(1024)(128)(4,1)S(1)}, s32[]{:S(2)}) async-start(s8[4718592]{0:T(1024)(128)(4,1)} %bitcast.6), calls=%async_computation | async-start | bytes 8388608
  98.8 17.0 %slice-start.1 = ((s8[4718592]{0:T(1024)(128)(4,1)}), s8[524288]{0:T(1024)(128)(4,1)S(1)}, s32[]{:S(2)}) async-start(s8[4718592]{0:T(1024)(128)(4,1)} %bitcast.6), calls=%async_computation.1 | async-start | bytes 1048576
  98.8 31.8 %collective-permute-start.17 = (bf16[4,192,256]{2,1,0:T(8,128)(2,1)S(1)}, bf16[4,192,256]{2,1,0:T(8,128)(2,1)S(1)}, u32[]{:S(2)}, u32[]{:S(2)}) collective-permute-start(bf16[4,192,256]{2,1,0:T(8,128)(2,1)S(1)} %get-tuple-element.60), channel_id=1, source_target_pairs={{1,0},{2,1},{3,2},{4,3},{5,4},{6,5},{7,6},{9,8},{10,9},{11,10},{12... | collective-permute-start | bytes 1179656 | tf_op jit(solution)/shard_map/ppermute | solution.py:323
  107.6 4.7 %collective-permute-start.11 = (f32[8,256]{1,0:T(8,128)S(1)}, f32[8,256]{1,0:T(8,128)S(1)}, u32[]{:S(2)}, u32[]{:S(2)}) collective-permute-start(f32[8,256]{1,0:T(8,128)S(1)} %get-tuple-element.64), channel_id=1, source_target_pairs={{8,0},{16,8},{24,16},{0,24},{9,1},{17,9},{25,17},{1,25},{10,2},{18... | collective-permute-start | bytes 24584 | tf_op jit(solution)/shard_map/ppermute | solution.py:317
  110.9 4.9 %collective-permute-start.12 = (f32[8,256]{1,0:T(8,128)S(1)}, f32[8,256]{1,0:T(8,128)S(1)}, u32[]{:S(2)}, u32[]{:S(2)}) collective-permute-start(f32[8,256]{1,0:T(8,128)S(1)} %get-tuple-element.65), channel_id=1, source_target_pairs={{0,8},{8,16},{16,24},{24,0},{1,9},{9,17},{17,25},{25,1},{2,10},{10... | collective-permute-start | bytes 24584 | tf_op jit(solution)/shard_map/ppermute | solution.py:317
  118.9 11.7 %copy-start.6 = (s32[9]{0:T(128)S(1)}, s32[9]{0:T(128)}, u32[]{:S(2)}) copy-start(s32[9]{0:T(128)} %cuts_ref.13) | copy-start | bytes 112
  122.0 14.2 %collective-permute-start.16 = (f32[8,256]{1,0:T(8,128)S(1)}, f32[8,256]{1,0:T(8,128)S(1)}, u32[]{:S(2)}, u32[]{:S(2)}) collective-permute-start(f32[8,256]{1,0:T(8,128)S(1)} %fusion.1), channel_id=1, source_target_pairs={{1,0},{2,1},{3,2},{4,3},{5,4},{6,5},{7,6},{0,7},{9,8},{10,9},{11,1... | collective-permute-start | bytes 24584 | tf_op jit(solution)/shard_map/ppermute | solution.py:317
  123.3 12.7 %collective-permute-start.15 = (f32[8,256]{1,0:T(8,128)S(1)}, f32[8,256]{1,0:T(8,128)S(1)}, u32[]{:S(2)}, u32[]{:S(2)}) collective-permute-start(f32[8,256]{1,0:T(8,128)S(1)} %fusion.1), channel_id=1, source_target_pairs={{0,1},{1,2},{2,3},{3,4},{4,5},{5,6},{6,7},{7,0},{8,9},{9,10},{10,1... | collective-permute-start | bytes 24584 | tf_op jit(solution)/shard_map/ppermute | solution.py:317
  130.6 2.3 %copy-start = (bf16[12,768,256]{2,1,0:T(8,128)(2,1)S(1)}, bf16[12,768,256]{2,1,0:T(8,128)(2,1)}, u32[]{:S(2)}) copy-start(bf16[12,768,256]{2,1,0:T(8,128)(2,1)} %get-tuple-element.55.swept_ref) | copy-start | bytes 14155780
